TPU v7x, 512 devices: a whole 4x8x8 slice. The times are simulated.
512 devices in a mesh: replica: 16 (over z_hi, x, core), section: 4 (over z_lo), tensor: 8 (over y).
Axes of the slice: x: 4, y: 8, z: 8 (z_hi: 2, z_lo: 4; z = z_hi * 4 + z_lo), core: 2. Of those that a mesh axis runs over, the one named last changes fastest.
Arguments:
- tokens: bfloat16 [16, 2, 256, 2048], P('replica', None, None, 'tensor'), may hold values from -6 to 6
- query_weight: bfloat16 [16, 4, 2048, 1024], P('replica', 'section', None, 'tensor'), may hold values from -5.524272 to 5.524272
- key_weight: bfloat16 [16, 4, 2048, 1024], P('replica', 'section', None, 'tensor'), may hold values from -0.13479223 to 0.13479223
- value_weight: bfloat16 [16, 4, 2048, 1024], P('replica', 'section', None, 'tensor'), may hold values from -0.125 to 0.125
- slow_output: bfloat16 [16, 4, 1024, 2048], P('replica', 'section', None, 'tensor'), may hold values from -0.75 to 0.75
- momentum: bfloat16 [16, 4, 1024, 2048], P('replica', 'section', None, 'tensor'), may hold values from -3 to 3
- out_grad: bfloat16 [16, 4, 2, 256, 2048], P('replica', 'section', None, None, 'tensor'), may hold values from -6 to 6
- route_keys: int32 [3, 2], replicated, may hold values from 0 to 15
- gossip_partner: int32 [4, 16], replicated, may hold values from 0 to 15, as said below
- positions: int32 [16, 2, 256], replicated, may hold values from 0 to 255, as said below
Outputs:
- section_outputs: bfloat16 [16, 4, 2, 256, 2048], P('replica', 'section', None, None, 'tensor')
- new_slow: bfloat16 [16, 4, 1024, 2048], P('replica', 'section', None, 'tensor')
- new_momentum: bfloat16 [16, 4, 1024, 2048], P('replica', 'section', None, 'tensor')
Inputs may be any that keep to these rules, and one draw needn't show every extreme that they name: For each section s, gossip_partner[s, r] = r XOR k_s for one k_s of 1 to 15, the same for every r. positions[r, m, 0] = 0, and each next entry is 0 (a new document) or one more than the one before.
All inputs are finite; a program needn't handle non-finite values.
Results may differ from a plain program's by a relative error of at most 0.018.
Values may be sent and summed in bfloat16 or wider, within the bound.
A program may use at most 64 MiB of HBM per device.

v0:
```python
import math

import jax
import jax.numpy as jnp
from jax import lax
from jax.sharding import PartitionSpec as P

HD = 128


inner_rate = 2.0
outer_rate = 0.7
outer_beta = 0.9
neg_fill = -1e30
norm_eps = 1e-05


def partner(block, axis, apart):
    count = lax.axis_size(axis)
    route = []
    for low in range(count):
        high = low | 1 << apart
        if high != low and high < count:
            route += [(low, high), (high, low)]
    return lax.ppermute(block, axis, route)


def shifted(array, axis, by):
    size = lax.axis_size(axis)
    pairs = [(i, i + by) for i in range(size) if 0 <= i + by < size]
    return lax.ppermute(array, axis, pairs)


def normalize(current):
    widened = current.astype(jnp.float32)
    return (
        widened * lax.rsqrt(jnp.mean(widened * widened, axis=-1, keepdims=True) + norm_eps)
    ).astype(jnp.bfloat16)


def attend(query_rows, key_rows, value_rows, doc_pos):
    length = query_rows.shape[0]
    scores = jnp.einsum(
        "qhd,khd->hqk", query_rows, key_rows, preferred_element_type=jnp.float32
    ) * HD ** (-0.5)
    row_ids = jnp.arange(length, dtype=jnp.int32)[:, None]
    col_ids = jnp.arange(length, dtype=jnp.int32)[None, :]
    allowed = (col_ids <= row_ids) & (row_ids - col_ids <= doc_pos[:, None])
    scores = jnp.where(allowed[None], scores, neg_fill)
    row_max = jnp.max(scores, axis=-1, keepdims=True)
    expo = jnp.exp(scores - row_max)
    probability = (expo / jnp.sum(expo, axis=-1, keepdims=True)).astype(jnp.bfloat16)
    mixed_rows = jnp.einsum(
        "hqk,khd->qhd", probability, value_rows, preferred_element_type=jnp.float32
    )
    return mixed_rows.reshape(length, -1).astype(jnp.bfloat16)


def section_layer(current, w_query, w_key, w_value, w_out, doc_pos):
    length = current.shape[0]
    gathered = lax.all_gather(current, "tensor", axis=1, tiled=True)
    normed = normalize(gathered)
    query_rows = (
        jnp.dot(normed, w_query, preferred_element_type=jnp.float32)
        .astype(jnp.bfloat16)
        .reshape(length, -1, HD)
    )
    key_rows = (
        jnp.dot(normed, w_key, preferred_element_type=jnp.float32)
        .astype(jnp.bfloat16)
        .reshape(length, -1, HD)
    )
    value_rows = (
        jnp.dot(normed, w_value, preferred_element_type=jnp.float32)
        .astype(jnp.bfloat16)
        .reshape(length, -1, HD)
    )
    local_heads = attend(query_rows, key_rows, value_rows, doc_pos)
    heads_all = lax.all_gather(local_heads, "tensor", axis=1, tiled=True)
    result = (
        current.astype(jnp.float32) + jnp.dot(heads_all, w_out, preferred_element_type=jnp.float32)
    ).astype(jnp.bfloat16)
    return (result, heads_all)


def route_mover(value, bit_index):
    return partner(value, "replica", bit_index)


def both_mover(value, bit_index):
    return partner(value, "replica", bit_index)


def xor_pairs(value, xor_mask, rounds, mover):
    for bit_index in range(rounds):
        bit_set = jnp.bitwise_and(jnp.right_shift(xor_mask, bit_index), 1) == 1
        moved = mover(value, bit_index)
        value = jnp.where(bit_set, moved, value)
    return value


def keep_slot(store, fresh, slot_index, active):
    previous = lax.dynamic_index_in_dim(store, slot_index, 0, keepdims=False)
    chosen = jnp.where(active, fresh, previous)
    return lax.dynamic_update_index_in_dim(store, chosen, slot_index, 0)


def pass_on(result, section_index, moment, sections, micro_count, route_keys, rounds):
    arrived = shifted(result, "section", 1)
    receiver_mask = route_keys[
        jnp.clip(section_index - 1, 0, sections - 2),
        jnp.clip(moment + 1 - section_index, 0, micro_count - 1),
    ]
    arrived = xor_pairs(arrived, receiver_mask, rounds, route_mover)
    return arrived


def shards(
    tokens,
    query_weight,
    key_weight,
    value_weight,
    slow_output,
    momentum,
    out_grad,
    route_keys,
    gossip_partner,
    positions,
):
    sections = lax.axis_size("section")
    section_index = lax.axis_index("section")
    replica_index = lax.axis_index("replica")
    rounds = lax.axis_size("replica").bit_length() - 1
    micro_count = tokens.shape[1]
    seq_len = tokens.shape[2]
    width_local = tokens.shape[3]
    w_query = query_weight[0, 0]
    w_key = key_weight[0, 0]
    w_value = value_weight[0, 0]
    w_out = slow_output[0, 0]
    own_momentum = momentum[0, 0]
    pair_mask = gossip_partner[section_index, 0]
    inbox = jnp.zeros((seq_len, width_local), jnp.bfloat16)
    out_store = jnp.zeros((micro_count, seq_len, width_local), jnp.bfloat16)
    heads_store = jnp.zeros((micro_count, seq_len, w_out.shape[0]), jnp.bfloat16)
    steps_total = micro_count + sections - 1
    for moment in range(steps_total):
        raw_slot = moment - section_index
        active = (raw_slot >= 0) & (raw_slot < micro_count)
        slot_index = jnp.clip(raw_slot, 0, micro_count - 1)
        current = jnp.where(section_index == 0, tokens[0, min(moment, micro_count - 1)], inbox)
        anchor = replica_index
        for earlier in range(sections - 1):
            anchor = jnp.where(
                earlier < section_index,
                jnp.bitwise_xor(anchor, route_keys[earlier, slot_index]),
                anchor,
            )
        doc_pos = positions[anchor, slot_index]
        result, heads_all = section_layer(current, w_query, w_key, w_value, w_out, doc_pos)
        out_store = keep_slot(out_store, result, slot_index, active)
        heads_store = keep_slot(heads_store, heads_all, slot_index, active)
        if moment + 1 < steps_total:
            inbox = pass_on(
                result, section_index, moment, sections, micro_count, route_keys, rounds
            )
    flat_heads = heads_store.reshape(micro_count * seq_len, -1)
    flat_grad = out_grad[0, 0].reshape(micro_count * seq_len, -1)
    grad_sum = jnp.einsum("th,td->hd", flat_heads, flat_grad, preferred_element_type=jnp.float32)
    delta_local = (grad_sum * (inner_rate / math.sqrt(micro_count * seq_len))).astype(jnp.bfloat16)
    packed = xor_pairs(jnp.stack([delta_local, own_momentum]), pair_mask, rounds, both_mover)
    mate_delta = packed[0]
    mate_momentum = packed[1]
    mean_delta = 0.5 * (delta_local.astype(jnp.float32) + mate_delta.astype(jnp.float32))
    momentum_next = (
        outer_beta * 0.5 * (own_momentum.astype(jnp.float32) + mate_momentum.astype(jnp.float32))
        + mean_delta
    )
    new_slow = w_out.astype(jnp.float32) - outer_rate * (outer_beta * momentum_next + mean_delta)
    return (
        out_store[None, None],
        new_slow.astype(jnp.bfloat16)[None, None],
        momentum_next.astype(jnp.bfloat16)[None, None],
    )


def solution(mesh):
    return jax.shard_map(
        shards,
        mesh=mesh,
        in_specs=(
            P("replica", None, None, "tensor"),
            P("replica", "section", None, "tensor"),
            P("replica", "section", None, "tensor"),
            P("replica", "section", None, "tensor"),
            P("replica", "section", None, "tensor"),
            P("replica", "section", None, "tensor"),
            P("replica", "section", None, None, "tensor"),
            P(),
            P(),
            P(),
        ),
        out_specs=(
            P("replica", "section", None, None, "tensor"),
            P("replica", "section", None, "tensor"),
            P("replica", "section", None, "tensor"),
        ),
        check_vma=False,
    )
```

profile of v0, /device:TPU:2, one launch (start us, length us, event | category | flops | bytes accessed | tf_op | source)
XLA Modules:
  0.0 659.6 jit_solution(4907038813990219277)
XLA Ops:
  22.1 35.2 %all-gather.20.cloned.1.call-done = bf16[1,1,256,2048]{3,2,1,0:T(8,128)(2,1)} async-done(((bf16[1,1,256,256]{3,2,1,0:T(8,128)(2,1)}), bf16[1,1,256,2048]{3,2,1,0:T(8,128)(2,1)}) %all-gather.20.cloned.1.call-update) | async-done | bytes 1048592 | tf_op jit(solution)/shard_map/all_gather | solution.py:61
  61.2 25.4 %all-gather.1 = bf16[256,1,1024]{0,2,1:T(8,128)(2,1)S(1)} all-gather(bf16[256,1,128]{0,2,1:T(8,128)(2,1)S(1)} %fusion.17), channel_id=3, replica_groups=mesh['replica'=16,'section'=4,'tensor'=8] {'tensor'}, dimensions={2}, use_global_device_ids=true | all-gather | bytes 589824 | tf_op jit(solution)/shard_map/all_gather | solution.py:79
  99.5 4.3 collective-permute-done.2
  112.2 7.1 %collective-permute-start.4 = (bf16[256,256]{1,0:T(8,128)(2,1)S(1)}, bf16[256,256]{1,0:T(8,128)(2,1)S(1)}, u32[]{:S(2)}, u32[]{:S(2)}) collective-permute-start(bf16[256,256]{1,0:T(8,128)(2,1)S(1)} %broadcast_select_fusion.15), channel_id=1, source_target_pairs={{0,256},{256,0},{32,288},{288,32},{64,320},{320,64},{96,352},{352,... | collective-permute-start | bytes 393224 | tf_op jit(solution)/shard_map/ppermute | solution.py:25
  123.8 42.4 %all-gather.12.cloned.1.call-done = bf16[256,2048]{1,0:T(8,128)(2,1)} async-done(((bf16[256,256]{1,0:T(8,128)(2,1)}), bf16[256,2048]{1,0:T(8,128)(2,1)}) %all-gather.12.cloned.1.call-update) | async-done | bytes 1048592 | tf_op jit(solution)/shard_map/all_gather | solution.py:61
  174.2 25.4 %all-gather.2 = bf16[256,1,1024]{0,2,1:T(8,128)(2,1)S(1)} all-gather(bf16[256,1,128]{0,2,1:T(8,128)(2,1)S(1)} %fusion.18), channel_id=4, replica_groups=mesh['replica'=16,'section'=4,'tensor'=8] {'tensor'}, dimensions={2}, use_global_device_ids=true | all-gather | bytes 589824 | tf_op jit(solution)/shard_map/all_gather | solution.py:79
  212.3 4.4 collective-permute-done.7
  225.2 7.1 %collective-permute-start.9 = (bf16[256,256]{1,0:T(8,128)(2,1)S(1)}, bf16[256,256]{1,0:T(8,128)(2,1)S(1)}, u32[]{:S(2)}, u32[]{:S(2)}) collective-permute-start(bf16[256,256]{1,0:T(8,128)(2,1)S(1)} %broadcast_select_fusion.12), channel_id=1, source_target_pairs={{0,256},{256,0},{32,288},{288,32},{64,320},{320,64},{96,352},{352,... | collective-permute-start | bytes 393224 | tf_op jit(solution)/shard_map/ppermute | solution.py:25
  236.8 42.4 %all-gather.14.cloned.1.call-done = bf16[256,2048]{1,0:T(8,128)(2,1)} async-done(((bf16[256,256]{1,0:T(8,128)(2,1)}), bf16[256,2048]{1,0:T(8,128)(2,1)}) %all-gather.14.cloned.1.call-update) | async-done | bytes 1048592 | tf_op jit(solution)/shard_map/all_gather | solution.py:61
  286.5 25.4 %all-gather.3 = bf16[256,1,1024]{0,2,1:T(8,128)(2,1)S(1)} all-gather(bf16[256,1,128]{0,2,1:T(8,128)(2,1)S(1)} %fusion.19), channel_id=5, replica_groups=mesh['replica'=16,'section'=4,'tensor'=8] {'tensor'}, dimensions={2}, use_global_device_ids=true | all-gather | bytes 589824 | tf_op jit(solution)/shard_map/all_gather | solution.py:79
  324.7 4.3 collective-permute-done.12
  329.0 4.0 collective-permute-start.13
  337.4 7.1 %collective-permute-start.14 = (bf16[256,256]{1,0:T(8,128)(2,1)S(1)}, bf16[256,256]{1,0:T(8,128)(2,1)S(1)}, u32[]{:S(2)}, u32[]{:S(2)}) collective-permute-start(bf16[256,256]{1,0:T(8,128)(2,1)S(1)} %broadcast_select_fusion.9), channel_id=1, source_target_pairs={{0,256},{256,0},{32,288},{288,32},{64,320},{320,64},{96,352},{352,... | collective-permute-start | bytes 393224 | tf_op jit(solution)/shard_map/ppermute | solution.py:25
  349.0 42.4 %all-gather.16.cloned.1.call-done = bf16[256,2048]{1,0:T(8,128)(2,1)} async-done(((bf16[256,256]{1,0:T(8,128)(2,1)}), bf16[256,2048]{1,0:T(8,128)(2,1)}) %all-gather.16.cloned.1.call-update) | async-done | bytes 1048592 | tf_op jit(solution)/shard_map/all_gather | solution.py:61
  398.7 25.4 %all-gather.4 = bf16[256,1,1024]{0,2,1:T(8,128)(2,1)S(1)} all-gather(bf16[256,1,128]{0,2,1:T(8,128)(2,1)S(1)} %fusion.20), channel_id=6, replica_groups=mesh['replica'=16,'section'=4,'tensor'=8] {'tensor'}, dimensions={2}, use_global_device_ids=true | all-gather | bytes 589824 | tf_op jit(solution)/shard_map/all_gather | solution.py:79
  438.0 4.3 collective-permute-done.17
  450.7 7.3 %collective-permute-start.19 = (bf16[256,256]{1,0:T(8,128)(2,1)S(1)}, bf16[256,256]{1,0:T(8,128)(2,1)S(1)}, u32[]{:S(2)}, u32[]{:S(2)}) collective-permute-start(bf16[256,256]{1,0:T(8,128)(2,1)S(1)} %broadcast_select_fusion.6), channel_id=1, source_target_pairs={{0,256},{256,0},{32,288},{288,32},{64,320},{320,64},{96,352},{352,... | collective-permute-start | bytes 393224 | tf_op jit(solution)/shard_map/ppermute | solution.py:25
  475.5 29.2 %all-gather.18.cloned.1.call-done = bf16[256,2048]{1,0:T(8,128)(2,1)} async-done(((bf16[256,256]{1,0:T(8,128)(2,1)}), bf16[256,2048]{1,0:T(8,128)(2,1)}) %all-gather.18.cloned.1.call-update) | async-done | bytes 1048592 | tf_op jit(solution)/shard_map/all_gather | solution.py:61
  510.8 25.4 %all-gather.5 = bf16[256,1,1024]{0,2,1:T(8,128)(2,1)S(1)} all-gather(bf16[256,1,128]{0,2,1:T(8,128)(2,1)S(1)} %fusion.21), channel_id=7, replica_groups=mesh['replica'=16,'section'=4,'tensor'=8] {'tensor'}, dimensions={2}, use_global_device_ids=true | all-gather | bytes 589824 | tf_op jit(solution)/shard_map/all_gather | solution.py:79
  547.6 24.0 %collective-permute-done.21 = bf16[2,1024,256]{2,1,0:T(8,128)(2,1)S(1)} collective-permute-done((bf16[2,1024,256]{2,1,0:T(8,128)(2,1)S(1)}, bf16[2,1024,256]{2,1,0:T(8,128)(2,1)S(1)}, u32[]{:S(2)}, u32[]{:S(2)}) %collective-permute-start.21) | collective-permute-done | bytes 1048608 | tf_op jit(solution)/shard_map/ppermute | solution.py:25
  571.9 4.0 collective-permute-start.22
  576.5 23.1 %collective-permute-done.22 = bf16[2,1024,256]{2,1,0:T(8,128)(2,1)S(1)} collective-permute-done((bf16[2,1024,256]{2,1,0:T(8,128)(2,1)S(1)}, bf16[2,1024,256]{2,1,0:T(8,128)(2,1)S(1)}, u32[]{:S(2)}, u32[]{:S(2)}) %collective-permute-start.22) | collective-permute-done | bytes 1048608 | tf_op jit(solution)/shard_map/ppermute | solution.py:25
  599.8 8.1 %collective-permute-start.23 = (bf16[2,1024,256]{2,1,0:T(8,128)(2,1)S(1)}, bf16[2,1024,256]{2,1,0:T(8,128)(2,1)S(1)}, u32[]{:S(2)}, u32[]{:S(2)}) collective-permute-start(bf16[2,1024,256]{2,1,0:T(8,128)(2,1)S(1)} %broadcast_select_fusion.2), channel_id=1, source_target_pairs={{0,256},{256,0},{32,288},{288,32},{64,320},{320,64},{96,352},{352,... | collective-permute-start | bytes 3145736 | tf_op jit(solution)/shard_map/ppermute | solution.py:25
  609.0 42.4 %collective-permute-done.23 = bf16[2,1024,256]{2,1,0:T(8,128)(2,1)S(1)} collective-permute-done((bf16[2,1024,256]{2,1,0:T(8,128)(2,1)S(1)}, bf16[2,1024,256]{2,1,0:T(8,128)(2,1)S(1)}, u32[]{:S(2)}, u32[]{:S(2)}) %collective-permute-start.23) | collective-permute-done | bytes 1048608 | tf_op jit(solution)/shard_map/ppermute | solution.py:25
  (185 shorter events, 152.3 us)
Async XLA Ops:
  7.2 50.1 %all-gather.20.cloned.1.call-start = ((), (), s32[]{:S(2)}) async-start(), calls=%async_computation.4 | async-start | bytes 1179648 | tf_op jit(solution)/shard_map/all_gather | solution.py:61
  8.9 157.3 %all-gather.12.cloned.1.call-start = ((), (), s32[]{:S(2)}) async-start(), calls=%async_computation | async-start | bytes 1179648 | tf_op jit(solution)/shard_map/all_gather | solution.py:61
  87.1 6.1 collective-permute-start
  96.4 7.4 %collective-permute-start.2 = (bf16[256,256]{1,0:T(8,128)(2,1)S(1)}, bf16[256,256]{1,0:T(8,128)(2,1)S(1)}, u32[]{:S(2)}, u32[]{:S(2)}) collective-permute-start(bf16[256,256]{1,0:T(8,128)(2,1)S(1)} %broadcast_select_fusion.13), channel_id=1, source_target_pairs={{0,64},{64,0},{32,96},{96,32},{128,192},{192,128},{160,224},{224,1... | collective-permute-start | bytes 393224 | tf_op jit(solution)/shard_map/ppermute | solution.py:25
  103.8 8.4 %collective-permute-start.3 = (bf16[256,256]{1,0:T(8,128)(2,1)S(1)}, bf16[256,256]{1,0:T(8,128)(2,1)S(1)}, u32[]{:S(2)}, u32[]{:S(2)}) collective-permute-start(bf16[256,256]{1,0:T(8,128)(2,1)S(1)} %broadcast_select_fusion.14), channel_id=1, source_target_pairs={{0,128},{128,0},{32,160},{160,32},{64,192},{192,64},{96,224},{224,... | collective-permute-start | bytes 393224 | tf_op jit(solution)/shard_map/ppermute | solution.py:25
  112.2 10.8 %collective-permute-start.4 = (bf16[256,256]{1,0:T(8,128)(2,1)S(1)}, bf16[256,256]{1,0:T(8,128)(2,1)S(1)}, u32[]{:S(2)}, u32[]{:S(2)}) collective-permute-start(bf16[256,256]{1,0:T(8,128)(2,1)S(1)} %broadcast_select_fusion.15), channel_id=1, source_target_pairs={{0,256},{256,0},{32,288},{288,32},{64,320},{320,64},{96,352},{352,... | collective-permute-start | bytes 393224 | tf_op jit(solution)/shard_map/ppermute | solution.py:25
  123.7 155.4 %all-gather.14.cloned.1.call-start = ((), (), s32[]{:S(2)}) async-start(), calls=%async_computation.1 | async-start | bytes 1179648 | tf_op jit(solution)/shard_map/all_gather | solution.py:61
  200.0 6.1 collective-permute-start.5
  209.3 7.4 %collective-permute-start.7 = (bf16[256,256]{1,0:T(8,128)(2,1)S(1)}, bf16[256,256]{1,0:T(8,128)(2,1)S(1)}, u32[]{:S(2)}, u32[]{:S(2)}) collective-permute-start(bf16[256,256]{1,0:T(8,128)(2,1)S(1)} %broadcast_select_fusion.10), channel_id=1, source_target_pairs={{0,64},{64,0},{32,96},{96,32},{128,192},{192,128},{160,224},{224,1... | collective-permute-start | bytes 393224 | tf_op jit(solution)/shard_map/ppermute | solution.py:25
  216.8 8.4 %collective-permute-start.8 = (bf16[256,256]{1,0:T(8,128)(2,1)S(1)}, bf16[256,256]{1,0:T(8,128)(2,1)S(1)}, u32[]{:S(2)}, u32[]{:S(2)}) collective-permute-start(bf16[256,256]{1,0:T(8,128)(2,1)S(1)} %broadcast_select_fusion.11), channel_id=1, source_target_pairs={{0,128},{128,0},{32,160},{160,32},{64,192},{192,64},{96,224},{224,... | collective-permute-start | bytes 393224 | tf_op jit(solution)/shard_map/ppermute | solution.py:25
  225.2 10.8 %collective-permute-start.9 = (bf16[256,256]{1,0:T(8,128)(2,1)S(1)}, bf16[256,256]{1,0:T(8,128)(2,1)S(1)}, u32[]{:S(2)}, u32[]{:S(2)}) collective-permute-start(bf16[256,256]{1,0:T(8,128)(2,1)S(1)} %broadcast_select_fusion.12), channel_id=1, source_target_pairs={{0,256},{256,0},{32,288},{288,32},{64,320},{320,64},{96,352},{352,... | collective-permute-start | bytes 393224 | tf_op jit(solution)/shard_map/ppermute | solution.py:25
  236.7 154.8 %all-gather.16.cloned.1.call-start = ((), (), s32[]{:S(2)}) async-start(), calls=%async_computation.2 | async-start | bytes 1179648 | tf_op jit(solution)/shard_map/all_gather | solution.py:61
  312.3 6.1 collective-permute-start.10
  321.6 7.4 %collective-permute-start.12 = (bf16[256,256]{1,0:T(8,128)(2,1)S(1)}, bf16[256,256]{1,0:T(8,128)(2,1)S(1)}, u32[]{:S(2)}, u32[]{:S(2)}) collective-permute-start(bf16[256,256]{1,0:T(8,128)(2,1)S(1)} %broadcast_select_fusion.7), channel_id=1, source_target_pairs={{0,64},{64,0},{32,96},{96,32},{128,192},{192,128},{160,224},{224,1... | collective-permute-start | bytes 393224 | tf_op jit(solution)/shard_map/ppermute | solution.py:25
  329.0 8.4 %collective-permute-start.13 = (bf16[256,256]{1,0:T(8,128)(2,1)S(1)}, bf16[256,256]{1,0:T(8,128)(2,1)S(1)}, u32[]{:S(2)}, u32[]{:S(2)}) collective-permute-start(bf16[256,256]{1,0:T(8,128)(2,1)S(1)} %broadcast_select_fusion.8), channel_id=1, source_target_pairs={{0,128},{128,0},{32,160},{160,32},{64,192},{192,64},{96,224},{224,... | collective-permute-start | bytes 393224 | tf_op jit(solution)/shard_map/ppermute | solution.py:25
  337.4 10.8 %collective-permute-start.14 = (bf16[256,256]{1,0:T(8,128)(2,1)S(1)}, bf16[256,256]{1,0:T(8,128)(2,1)S(1)}, u32[]{:S(2)}, u32[]{:S(2)}) collective-permute-start(bf16[256,256]{1,0:T(8,128)(2,1)S(1)} %broadcast_select_fusion.9), channel_id=1, source_target_pairs={{0,256},{256,0},{32,288},{288,32},{64,320},{320,64},{96,352},{352,... | collective-permute-start | bytes 393224 | tf_op jit(solution)/shard_map/ppermute | solution.py:25
  348.9 155.8 %all-gather.18.cloned.1.call-start = ((), (), s32[]{:S(2)}) async-start(), calls=%async_computation.3 | async-start | bytes 1179648 | tf_op jit(solution)/shard_map/all_gather | solution.py:61
  425.5 6.1 collective-permute-start.15
  434.9 7.4 %collective-permute-start.17 = (bf16[256,256]{1,0:T(8,128)(2,1)S(1)}, bf16[256,256]{1,0:T(8,128)(2,1)S(1)}, u32[]{:S(2)}, u32[]{:S(2)}) collective-permute-start(bf16[256,256]{1,0:T(8,128)(2,1)S(1)} %broadcast_select_fusion.4), channel_id=1, source_target_pairs={{0,64},{64,0},{32,96},{96,32},{128,192},{192,128},{160,224},{224,1... | collective-permute-start | bytes 393224 | tf_op jit(solution)/shard_map/ppermute | solution.py:25
  442.3 8.4 %collective-permute-start.18 = (bf16[256,256]{1,0:T(8,128)(2,1)S(1)}, bf16[256,256]{1,0:T(8,128)(2,1)S(1)}, u32[]{:S(2)}, u32[]{:S(2)}) collective-permute-start(bf16[256,256]{1,0:T(8,128)(2,1)S(1)} %broadcast_select_fusion.5), channel_id=1, source_target_pairs={{0,128},{128,0},{32,160},{160,32},{64,192},{192,64},{96,224},{224,... | collective-permute-start | bytes 393224 | tf_op jit(solution)/shard_map/ppermute | solution.py:25
  450.7 10.8 %collective-permute-start.19 = (bf16[256,256]{1,0:T(8,128)(2,1)S(1)}, bf16[256,256]{1,0:T(8,128)(2,1)S(1)}, u32[]{:S(2)}, u32[]{:S(2)}) collective-permute-start(bf16[256,256]{1,0:T(8,128)(2,1)S(1)} %broadcast_select_fusion.6), channel_id=1, source_target_pairs={{0,256},{256,0},{32,288},{288,32},{64,320},{320,64},{96,352},{352,... | collective-permute-start | bytes 393224 | tf_op jit(solution)/shard_map/ppermute | solution.py:25
  544.5 27.1 %collective-permute-start.21 = (bf16[2,1024,256]{2,1,0:T(8,128)(2,1)S(1)}, bf16[2,1024,256]{2,1,0:T(8,128)(2,1)S(1)}, u32[]{:S(2)}, u32[]{:S(2)}) collective-permute-start(bf16[2,1024,256]{2,1,0:T(8,128)(2,1)S(1)} %broadcast_select_fusion), channel_id=1, source_target_pairs={{0,64},{64,0},{32,96},{96,32},{128,192},{192,128},{160,224},{224,1... | collective-permute-start | bytes 3145736 | tf_op jit(solution)/shard_map/ppermute | solution.py:25
  571.9 27.8 %collective-permute-start.22 = (bf16[2,1024,256]{2,1,0:T(8,128)(2,1)S(1)}, bf16[2,1024,256]{2,1,0:T(8,128)(2,1)S(1)}, u32[]{:S(2)}, u32[]{:S(2)}) collective-permute-start(bf16[2,1024,256]{2,1,0:T(8,128)(2,1)S(1)} %broadcast_select_fusion.1), channel_id=1, source_target_pairs={{0,128},{128,0},{32,160},{160,32},{64,192},{192,64},{96,224},{224,... | collective-permute-start | bytes 3145736 | tf_op jit(solution)/shard_map/ppermute | solution.py:25
  599.8 51.7 %collective-permute-start.23 = (bf16[2,1024,256]{2,1,0:T(8,128)(2,1)S(1)}, bf16[2,1024,256]{2,1,0:T(8,128)(2,1)S(1)}, u32[]{:S(2)}, u32[]{:S(2)}) collective-permute-start(bf16[2,1024,256]{2,1,0:T(8,128)(2,1)S(1)} %broadcast_select_fusion.2), channel_id=1, source_target_pairs={{0,256},{256,0},{32,288},{288,32},{64,320},{320,64},{96,352},{352,... | collective-permute-start | bytes 3145736 | tf_op jit(solution)/shard_map/ppermute | solution.py:25
  (30 other events, 402.4 us)
Sparse Core Ops, SparseCore 0:
  10.6 46.6 all-gather.19
  123.9 42.3 all-gather.11
  236.8 42.3 all-gather.13
  349.0 42.3 all-gather.15
  462.3 42.3 all-gather.17
where the time goes:
time: 662 us; the launch traced here: 660 us
  waiting for transfers between devices  339 us (51%)
  blocking collectives  127 us (19%)
  starting transfers between devices  93 us (14%)
  between operations  36.8 us (6%)
  matrix products  26.2 us (4%)
  other arithmetic  20.3 us (3%)
  local copies, waits for them, and re-layouts  16.7 us (3%)
    all_gather x5, waiting for transfers between devices, section_layer(): gathered = lax.all_gather(current, 'tensor', axis=1, tiled=True)  192 us
    ppermute x20, waiting for transfers between devices, partner(): return lax.ppermute(block, axis, route)  138 us
    all_gather x5, blocking collectives, section_layer(): heads_all = lax.all_gather(local_heads, 'tensor', axis=1, tiled=True)  127 us
    ppermute x20, starting transfers between devices, partner(): return lax.ppermute(block, axis, route)  78.5 us
    ppermute x4, starting transfers between devices, shifted(): return lax.ppermute(array, axis, pairs)  14.2 us
  transfers between devices with their start and end apart: 29, of which 29 were waited for; matrix products, arithmetic and copies ran while one was open for 3% of the time, Pallas kernels for 0%

commit v1 on v0

v1 whole, which is shorter than its diff:
```python
import functools
import math

import jax
import jax.numpy as jnp
from jax import lax
from jax.experimental import pallas as pl
from jax.experimental.pallas import tpu as pltpu
from jax.sharding import PartitionSpec as P

MESH = pl.DeviceIdType.MESH

HD = 128
CHUNKS = 4
inner_rate = 2.0
outer_rate = 0.7
outer_beta = 0.9
neg_fill = -1e30
norm_eps = 1e-05


def bit_groups(replicas):
    bits = replicas.bit_length() - 1
    first = [0] + ([3] if bits > 3 else [])
    second = [b for b in range(bits) if b not in first]
    return first, second


def spread(index, bits):
    return sum(((index >> i) & 1) << b for i, b in enumerate(bits))


def choose(blocks, mask, bits):
    for b in bits:
        flipped = jnp.bitwise_and(jnp.right_shift(mask, b), 1) == 1
        blocks = [jnp.where(flipped, odd, even) for even, odd in zip(blocks[::2], blocks[1::2])]
    return blocks[0]


def kernel(
    cfg,
    route_ref, gossip_ref, pos_ref, tok_ref, wq_ref, wk_ref, wv_ref, wo_ref, mom_ref, grad_ref,
    out_ref, slow_ref, newm_ref,
    first_buf, second_buf, x_buf, heads_buf, k_buf, v_buf,
    delta_buf, mom_a, mom_b, mom_d, del_a, del_b, del_d,
    s_first, r_first, s_second, r_second, s_x, r_x, s_h, r_h,
    s_ma, r_ma, s_mb, r_mb, s_da, r_da, s_db, r_db,
):
    replicas, sections, tensors, units, chunks, rows = cfg
    micros = units // chunks
    first_bits, second_bits = bit_groups(replicas)
    n_first, n_second = 1 << len(first_bits), 1 << len(second_bits)
    rep, sec, ten = lax.axis_index("replica"), lax.axis_index("section"), lax.axis_index("tensor")
    last = sections - 1

    def flip(mask):
        return jnp.bitwise_xor(rep, mask) if mask else rep

    barrier = pltpu.get_barrier_semaphore()
    greeted = 0
    for mask in range(1, replicas):
        pl.semaphore_signal(barrier, inc=1, device_id=(flip(mask), sec, ten), device_id_type=MESH)
        greeted += 1
    for off in range(1, tensors):
        pl.semaphore_signal(
            barrier, inc=1, device_id=(rep, sec, lax.rem(ten + off, tensors)), device_id_type=MESH
        )
        greeted += 1
    for way in (1, sections - 1):
        for e in range(n_first):
            pl.semaphore_signal(
                barrier,
                inc=1,
                device_id=(flip(spread(e, first_bits)), lax.rem(sec + way, sections), ten),
                device_id_type=MESH,
            )
            greeted += 1

    k_buf[...] = jnp.zeros_like(k_buf)
    v_buf[...] = jnp.zeros_like(v_buf)
    pl.semaphore_wait(barrier, greeted)

    def send(src, dst, s_sem, r_sem, where):
        return pltpu.make_async_remote_copy(
            src_ref=src, dst_ref=dst, send_sem=s_sem, recv_sem=r_sem, device_id=where, device_id_type=MESH
        )

    def await_bytes(ref, sem):
        pltpu.make_async_copy(ref, ref, sem).wait()

    pair = gossip_ref[sec, 0]

    def swap_start(src, a, s_sem, r_sem):
        for c in range(1, replicas):
            send(src.at[c], a.at[c], s_sem, r_sem, (flip(c), sec, ten)).start()
        a[0] = src[0]

    def swap_turn(a, b, d, rs_a, s_sem, r_sem):
        await_bytes(a.at[pl.ds(1, replicas - 1)], rs_a)
        for j in range(replicas):
            block = a[jnp.bitwise_xor(pair, j)]
            if j == 0:
                d[0] = block
            else:
                b[j] = block
                send(b.at[j], d.at[j], s_sem, r_sem, (flip(j), sec, ten)).start()

    swap_start(mom_ref, mom_a, s_ma, r_ma)

    @pl.when(sec != 0)
    def _():
        swap_turn(mom_a, mom_b, mom_d, r_ma, s_mb, r_mb)

    def relay_mask(unit):
        return route_ref[jnp.maximum(sec - 1, 0), unit // chunks]

    def stage_pick(unit):
        await_bytes(first_buf.at[unit], r_first.at[unit])
        second_buf[unit, 0] = choose([first_buf[unit, e] for e in range(n_first)], relay_mask(unit), first_bits)
        for j in range(1, n_second):
            send(
                second_buf.at[unit, 0], second_buf.at[unit, j], s_second.at[unit], r_second.at[unit],
                (flip(spread(j, second_bits)), sec, ten),
            ).start()

    def stage_gather(unit):
        @pl.when(sec == 0)
        def _():
            x_buf[unit, ten] = tok_ref[unit]

        @pl.when(sec != 0)
        def _():
            await_bytes(second_buf.at[unit, pl.ds(1, n_second - 1)], r_second.at[unit])
            x_buf[unit, ten] = choose([second_buf[unit, j] for j in range(n_second)], relay_mask(unit), second_bits)

        for off in [o for d in range(tensors // 2, 0, -1) for o in sorted({d, tensors - d})]:
            send(
                x_buf.at[unit, ten], x_buf.at[unit, ten], s_x.at[unit], r_x.at[unit],
                (rep, sec, lax.rem(ten + off, tensors)),
            ).start()

    def stage_attend(unit):
        micro, chunk = unit // chunks, lax.rem(unit, chunks)
        anchor = rep
        for earlier in range(last):
            anchor = jnp.bitwise_xor(anchor, jnp.where(earlier < sec, route_ref[earlier, micro], 0))
        await_bytes(x_buf.at[unit, pl.ds(0, tensors - 1)], r_x.at[unit])
        width = x_buf.shape[3]
        total = jnp.zeros((rows, 3 * HD), jnp.float32)
        squares = jnp.zeros((rows, width), jnp.float32)
        for b in range(tensors):
            block = x_buf[unit, b]
            deep = pl.ds(b * width, width)
            weight = jnp.concatenate([wq_ref[deep, :], wk_ref[deep, :], wv_ref[deep, :]], axis=1)
            total += jnp.dot(block, weight, preferred_element_type=jnp.float32)
            wide = block.astype(jnp.float32)
            squares += wide * wide
        mean = jnp.sum(squares, axis=1, keepdims=True) * (1.0 / (width * tensors))
        qkv = (total * lax.rsqrt(mean + norm_eps)).astype(jnp.bfloat16)
        k_buf[micro, chunk] = qkv[:, HD : 2 * HD]
        v_buf[micro, chunk] = qkv[:, 2 * HD :]
        length = chunks * rows
        keys = k_buf[micro].reshape(length, HD)
        values = v_buf[micro].reshape(length, HD)
        scores = lax.dot_general(
            qkv[:, :HD], keys, (((1,), (1,)), ((), ())), preferred_element_type=jnp.float32
        ) * HD ** (-0.5)
        row_ids = lax.broadcasted_iota(jnp.int32, (rows, length), 0) + chunk * rows
        col_ids = lax.broadcasted_iota(jnp.int32, (rows, length), 1)
        here = pos_ref[anchor, pl.ds(micro, 1), :]
        doc_pos = jnp.sum(
            jnp.where(row_ids == col_ids, jnp.broadcast_to(here, (rows, length)), 0), axis=1, keepdims=True
        )
        allowed = (col_ids <= row_ids) & (row_ids - col_ids <= doc_pos)
        scores = jnp.where(allowed, scores, neg_fill)
        expo = jnp.exp(scores - jnp.max(scores, axis=1, keepdims=True))
        probability = (expo / jnp.sum(expo, axis=1, keepdims=True)).astype(jnp.bfloat16)
        heads = jnp.dot(probability, values, preferred_element_type=jnp.float32)
        heads_buf[unit, ten] = heads.astype(jnp.bfloat16)
        for off in [o for d in range(tensors // 2, 0, -1) for o in sorted({d, tensors - d})]:
            send(
                heads_buf.at[unit, ten], heads_buf.at[unit, ten], s_h.at[unit], r_h.at[unit],
                (rep, sec, lax.rem(ten + off, tensors)),
            ).start()

    def stage_out(unit):
        await_bytes(heads_buf.at[unit, pl.ds(0, tensors - 1)], r_h.at[unit])
        total = x_buf[unit, ten].astype(jnp.float32)
        for b in range(0, tensors, 2):
            both = jnp.concatenate([heads_buf[unit, b], heads_buf[unit, b + 1]], axis=1)
            total += jnp.dot(both, wo_ref[pl.ds(b * HD, 2 * HD), :], preferred_element_type=jnp.float32)
        out_ref[unit] = total.astype(jnp.bfloat16)

        @pl.when(sec != last)
        def _():
            for e in range(n_first - 1, -1, -1):
                send(
                    out_ref.at[unit], first_buf.at[unit, e], s_first.at[unit], r_first.at[unit],
                    (flip(spread(e, first_bits)), lax.rem(sec + 1, sections), ten),
                ).start()

    def tick(t, carry):
        @pl.when((sec != 0) & (t < units))
        def _():
            stage_pick(t)

        @pl.when((t >= 2) & (t < units + 2))
        def _():
            stage_attend(t - 2)

        @pl.when(t < units)
        def _():
            stage_gather(t)

        @pl.when(t >= 3)
        def _():
            stage_out(t - 3)

        return carry

    lax.fori_loop(0, units + 3, tick, 0)

    piece = delta_buf.shape[1]
    per_head = HD // piece if piece <= HD else 1
    scale = inner_rate / math.sqrt(units * rows)

    def delta_step(h, carry):
        mine = heads_buf[:, h].reshape(units * rows, HD)
        grad = lax.dot_general(
            mine, grad_ref[...], (((0,), (0,)), ((), ())), preferred_element_type=jnp.float32
        )
        delta = (grad * scale).astype(jnp.bfloat16)
        for q in range(per_head):
            delta_buf[h * per_head + q] = delta[q * piece : (q + 1) * piece]
        return carry

    lax.fori_loop(0, tensors, delta_step, 0)
    swap_start(delta_buf, del_a, s_da, r_da)

    @pl.when(sec == 0)
    def _():
        swap_turn(mom_a, mom_b, mom_d, r_ma, s_mb, r_mb)

    swap_turn(del_a, del_b, del_d, r_da, s_db, r_db)
    await_bytes(mom_d.at[pl.ds(1, replicas - 1)], r_mb)
    await_bytes(del_d.at[pl.ds(1, replicas - 1)], r_db)

    def update(c, carry):
        there = jnp.bitwise_xor(pair, c)
        mean_delta = 0.5 * (delta_buf[c].astype(jnp.float32) + del_d[there].astype(jnp.float32))
        both = mom_ref[c].astype(jnp.float32) + mom_d[there].astype(jnp.float32)
        momentum_next = outer_beta * 0.5 * both + mean_delta
        old = wo_ref[pl.ds(pl.multiple_of(c * piece, piece), piece), :].astype(jnp.float32)
        slow_ref[c] = (old - outer_rate * (outer_beta * momentum_next + mean_delta)).astype(jnp.bfloat16)
        newm_ref[c] = momentum_next.astype(jnp.bfloat16)
        return carry

    lax.fori_loop(0, replicas, update, 0)

    await_bytes(mom_a.at[pl.ds(1, replicas - 1)], s_ma)
    await_bytes(mom_a.at[pl.ds(1, replicas - 1)], s_mb)
    await_bytes(mom_a.at[pl.ds(1, replicas - 1)], s_da)
    await_bytes(mom_a.at[pl.ds(1, replicas - 1)], s_db)

    def drain(u, carry):
        await_bytes(x_buf.at[u, pl.ds(0, tensors - 1)], s_x.at[u])
        await_bytes(heads_buf.at[u, pl.ds(0, tensors - 1)], s_h.at[u])

        @pl.when(sec != 0)
        def _():
            await_bytes(second_buf.at[u, pl.ds(1, n_second - 1)], s_second.at[u])

        @pl.when(sec != last)
        def _():
            await_bytes(first_buf.at[u], s_first.at[u])

        return carry

    lax.fori_loop(0, units, drain, 0)


def shards(sizes, tokens, query_weight, key_weight, value_weight, slow_output, momentum, out_grad, route_keys,
           gossip_partner, positions):
    replicas, sections, tensors = sizes
    _, micros, length, width = tokens.shape
    chunks = CHUNKS
    rows = length // chunks
    units = micros * chunks
    wo = slow_output[0, 0]
    high = wo.shape[0]
    piece = high // replicas
    first_bits, second_bits = bit_groups(replicas)
    n_first, n_second = 1 << len(first_bits), 1 << len(second_bits)
    bf = jnp.bfloat16
    swap = pltpu.VMEM((replicas, piece, width), bf)
    dma = pltpu.SemaphoreType.DMA
    vmem = pl.BlockSpec(memory_space=pltpu.VMEM)
    smem = pl.BlockSpec(memory_space=pltpu.SMEM)
    cfg = (replicas, sections, tensors, units, chunks, rows)
    out, slow, newm = pl.pallas_call(
        functools.partial(kernel, cfg),
        out_shape=(
            jax.ShapeDtypeStruct((units, rows, width), bf),
            jax.ShapeDtypeStruct((replicas, piece, width), bf),
            jax.ShapeDtypeStruct((replicas, piece, width), bf),
        ),
        in_specs=[smem, smem] + [vmem] * 8,
        out_specs=(vmem, vmem, vmem),
        scratch_shapes=[
            pltpu.VMEM((units, n_first, rows, width), bf),
            pltpu.VMEM((units, n_second, rows, width), bf),
            pltpu.VMEM((units, tensors, rows, width), bf),
            pltpu.VMEM((units, tensors, rows, HD), bf),
            pltpu.VMEM((micros, chunks, rows, HD), bf),
            pltpu.VMEM((micros, chunks, rows, HD), bf),
            swap, swap, swap, swap, swap, swap, swap,
        ]
        + [dma((units,))] * 8
        + [dma] * 8,
        compiler_params=pltpu.CompilerParams(
            collective_id=0, has_side_effects=True, vmem_limit_bytes=40 * 1024 * 1024
        ),
    )(
        route_keys, gossip_partner, positions, tokens.reshape(units, rows, width),
        query_weight[0, 0], key_weight[0, 0], value_weight[0, 0], wo,
        momentum.reshape(replicas, piece, width), out_grad.reshape(units * rows, width),
    )
    return (
        out.reshape(1, 1, micros, length, width),
        slow.reshape(1, 1, high, width),
        newm.reshape(1, 1, high, width),
    )


def solution(mesh):
    sizes = tuple(mesh.shape[a] for a in ("replica", "section", "tensor"))
    weights = P("replica", "section", None, "tensor")
    return jax.shard_map(
        functools.partial(shards, sizes),
        mesh=mesh,
        in_specs=(
            P("replica", None, None, "tensor"),
            weights, weights, weights, weights, weights,
            P("replica", "section", None, None, "tensor"),
            P(), P(), P(),
        ),
        out_specs=(P("replica", "section", None, None, "tensor"), weights, weights),
        check_vma=False,
    )
```

time: 662 us -> 222 us (0.34)
  the two profiles are of different devices: /device:TPU:2 before, /device:TPU:193 now
where the time goes in v1:
time: 222 us
  Pallas kernels  210 us (95%)
  local copies, waits for them, and re-layouts  10.9 us (5%)
    pallas_call x1, Pallas kernels, shards(): pl.pallas_call(functools.partial(kernel, cfg), out_shape=(jax.ShapeDtypeS...  210 us
    unnamed x24, local copies, waits for them, and re-layouts  10.9 us

profile of v1, /device:TPU:193, one launch (start us, length us, event | category | flops | bytes accessed | tf_op | source)
XLA Modules:
  0.0 222.0 jit_solution(5595728164517307120)
XLA Ops:
  0.6 0.0 copy-start.9
  0.6 0.0 copy-start.8
  0.7 0.7 copy-done.9
  1.3 0.1 copy.13.route_ref
  1.4 0.0 copy-done.8
  1.4 0.0 copy-start
  1.4 1.0 copy-done
  2.4 0.0 copy-start.1
  2.5 1.0 copy-done.1
  3.5 0.0 copy-start.2
  3.5 1.0 copy-done.2
  4.5 1.0 copy-done.3
  5.6 0.0 copy-start.4
  5.6 1.0 copy-done.4
  6.6 0.0 copy-start.5
  6.6 0.9 copy-done.5
  7.6 0.0 copy-start.6
  7.6 0.9 copy-done.6
  8.5 0.0 copy-start.7
  8.5 0.8 copy-done.7
  9.3 210.4 %shard_map.121 = (bf16[8,64,256]{2,1,0:T(8,128)(2,1)S(1)}, bf16[16,64,256]{2,1,0:T(8,128)(2,1)S(1)}, bf16[16,64,256]{2,1,0:T(8,128)(2,1)S(1)}) custom-call(s32[3,2]{1,0:T(4,128)S(1)} %copy.13.route_ref, s32[4,16]{1,0:T(4,128)S(1)} %copy-done.8, s32[16,2,256]{2,1,0:T(2,128)S(1)} %copy-done.7, bf16[8,64,256]{2,1,0:T(8,128)(2,1)S(1)} %bitcast.17, ...), custom_call_target="tpu_custom_call" | custom-call | tf_op jit(solution)/shard_map/pallas_call | solution.py:300
  219.7 0.7 copy.17
  220.4 0.8 copy.18
  221.2 0.8 copy.19
  (1 shorter events, 0.0 us)
Async XLA Ops:
  0.6 0.7 copy-start.9
  0.6 0.8 copy-start.8
  1.4 1.0 copy-start
  2.4 1.0 copy-start.1
  3.5 1.0 copy-start.2
  4.5 1.0 copy-start.3
  5.6 1.0 copy-start.4
  6.6 0.9 copy-start.5
  7.6 0.9 copy-start.6
  8.5 0.8 copy-start.7

commit v2 on v1

--- a/solution.py
+++ b/solution.py
@@ -11,7 +11,9 @@
 MESH = pl.DeviceIdType.MESH
 
 HD = 128
-CHUNKS = 4
+CHUNKS = 8
+PARTS = 2
+SCHEDULE = (("pick", 0), ("hand_x", 3), ("hand_heads", 6), ("gather", 1), ("attend", 4), ("out", 7))
 inner_rate = 2.0
 outer_rate = 0.7
 outer_beta = 0.9
@@ -39,15 +41,16 @@
 
 def kernel(
     cfg,
-    route_ref, gossip_ref, pos_ref, tok_ref, wq_ref, wk_ref, wv_ref, wo_ref, mom_ref, grad_ref,
+    route_ref, gossip_ref, pos_in, tok_in, wq_in, wk_in, wv_in, wo_in, mom_in, grad_in,
     out_ref, slow_ref, newm_ref,
+    pos_ref, tok_ref, w_ref, wo_ref, mom_ref, grad_ref, grad_acc,
     first_buf, second_buf, x_buf, heads_buf, k_buf, v_buf,
-    delta_buf, mom_a, mom_b, mom_d, del_a, del_b, del_d,
+    delta_buf, mom_b, mom_d, del_b, del_d, landed,
     s_first, r_first, s_second, r_second, s_x, r_x, s_h, r_h,
-    s_ma, r_ma, s_mb, r_mb, s_da, r_da, s_db, r_db,
+    s_ma, r_ma, s_mb, r_mb, s_da, r_da, s_db, r_db, s_in,
 ):
     replicas, sections, tensors, units, chunks, rows = cfg
-    micros = units // chunks
+    mom_a, del_a = landed[:PARTS], landed[PARTS:]
     first_bits, second_bits = bit_groups(replicas)
     n_first, n_second = 1 << len(first_bits), 1 << len(second_bits)
     rep, sec, ten = lax.axis_index("replica"), lax.axis_index("section"), lax.axis_index("tensor")
@@ -55,6 +58,24 @@
 
     def flip(mask):
         return jnp.bitwise_xor(rep, mask) if mask else rep
+
+    loads = [
+        pltpu.make_async_copy(src, dst, s_in.at[i])
+        for i, (src, dst) in enumerate(
+            (
+                (tok_in, tok_ref),
+                (pos_in, pos_ref),
+                (wq_in, w_ref.at[:, pl.ds(0, HD)]),
+                (wk_in, w_ref.at[:, pl.ds(HD, HD)]),
+                (wv_in, w_ref.at[:, pl.ds(2 * HD, HD)]),
+                (wo_in, wo_ref),
+                (mom_in, mom_ref),
+                (grad_in, grad_ref),
+            )
+        )
+    ]
+    for load in loads:
+        load.start()
 
     barrier = pltpu.get_barrier_semaphore()
     greeted = 0
@@ -78,6 +99,8 @@
 
     k_buf[...] = jnp.zeros_like(k_buf)
     v_buf[...] = jnp.zeros_like(v_buf)
+    for load in loads:
+        load.wait()
     pl.semaphore_wait(barrier, greeted)
 
     def send(src, dst, s_sem, r_sem, where):
@@ -90,20 +113,30 @@
 
     pair = gossip_ref[sec, 0]
 
+    part = mom_ref.shape[1] // PARTS
+    outward = sorted(range(1, replicas), key=lambda c: (-(c >> 3), -((c >> 1) & 3 == 2), -(c >> 1)))
+
+    def rows_of(p):
+        return pl.ds(p * part, part)
+
     def swap_start(src, a, s_sem, r_sem):
-        for c in range(1, replicas):
-            send(src.at[c], a.at[c], s_sem, r_sem, (flip(c), sec, ten)).start()
-        a[0] = src[0]
+        for p in range(PARTS):
+            for c in outward:
+                send(
+                    src.at[c, rows_of(p)], a[p].at[c], s_sem.at[p], r_sem.at[p], (flip(c), sec, ten)
+                ).start()
+            a[p][0] = src[0, rows_of(p)]
 
     def swap_turn(a, b, d, rs_a, s_sem, r_sem):
-        await_bytes(a.at[pl.ds(1, replicas - 1)], rs_a)
-        for j in range(replicas):
-            block = a[jnp.bitwise_xor(pair, j)]
-            if j == 0:
-                d[0] = block
-            else:
-                b[j] = block
-                send(b.at[j], d.at[j], s_sem, r_sem, (flip(j), sec, ten)).start()
+        for p in range(PARTS):
+            await_bytes(a[p].at[pl.ds(1, replicas - 1)], rs_a.at[p])
+            for j in outward:
+                b[j, rows_of(p)] = a[p][jnp.bitwise_xor(pair, j)]
+                send(b.at[j, rows_of(p)], d.at[j, rows_of(p)], s_sem.at[p], r_sem.at[p], (flip(j), sec, ten)).start()
+            d[0, rows_of(p)] = a[p][pair]
+
+    def await_part(a, p, sem):
+        await_bytes(a.at[pl.ds(1, replicas - 1), rows_of(p)], sem.at[p])
 
     swap_start(mom_ref, mom_a, s_ma, r_ma)
 
@@ -113,6 +146,29 @@
 
     def relay_mask(unit):
         return route_ref[jnp.maximum(sec - 1, 0), unit // chunks]
+
+    def beside(off):
+        return lax.rem(ten + off + tensors, tensors)
+
+    def near_and_far(buf, unit, s_sem, r_sem):
+        for kind, offs in ((1, (2, -2)), (0, (1, -1))):
+            for off in offs:
+                send(
+                    buf.at[unit, ten], buf.at[unit, ten], s_sem.at[unit, kind], r_sem.at[unit, kind],
+                    (rep, sec, beside(off)),
+                ).start()
+
+    def hand_on(buf, unit, s_sem, r_sem):
+        await_bytes(buf.at[unit, pl.ds(0, 2)], r_sem.at[unit, 1])
+        for way in (1, -1):
+            block = buf.at[unit, beside(-2 * way)]
+            half = block.at[pl.ds(0 if way == 1 else rows // 2, rows // 2)]
+            for src, off in ((half, 2 * way), (block, way)):
+                send(src, src, s_sem.at[unit, 2], r_sem.at[unit, 2], (rep, sec, beside(off))).start()
+
+    def await_rest(buf, unit, r_sem):
+        await_bytes(buf.at[unit, pl.ds(0, 2)], r_sem.at[unit, 0])
+        await_bytes(buf.at[unit, pl.ds(0, 3)], r_sem.at[unit, 2])
 
     def stage_pick(unit):
         await_bytes(first_buf.at[unit], r_first.at[unit])
@@ -133,26 +189,27 @@
             await_bytes(second_buf.at[unit, pl.ds(1, n_second - 1)], r_second.at[unit])
             x_buf[unit, ten] = choose([second_buf[unit, j] for j in range(n_second)], relay_mask(unit), second_bits)
 
-        for off in [o for d in range(tensors // 2, 0, -1) for o in sorted({d, tensors - d})]:
-            send(
-                x_buf.at[unit, ten], x_buf.at[unit, ten], s_x.at[unit], r_x.at[unit],
-                (rep, sec, lax.rem(ten + off, tensors)),
-            ).start()
+        near_and_far(x_buf, unit, s_x, r_x)
+
+    def stage_hand_x(unit):
+        hand_on(x_buf, unit, s_x, r_x)
+
+    def stage_hand_heads(unit):
+        hand_on(heads_buf, unit, s_h, r_h)
 
     def stage_attend(unit):
         micro, chunk = unit // chunks, lax.rem(unit, chunks)
         anchor = rep
         for earlier in range(last):
             anchor = jnp.bitwise_xor(anchor, jnp.where(earlier < sec, route_ref[earlier, micro], 0))
-        await_bytes(x_buf.at[unit, pl.ds(0, tensors - 1)], r_x.at[unit])
+        await_rest(x_buf, unit, r_x)
         width = x_buf.shape[3]
         total = jnp.zeros((rows, 3 * HD), jnp.float32)
         squares = jnp.zeros((rows, width), jnp.float32)
         for b in range(tensors):
             block = x_buf[unit, b]
             deep = pl.ds(b * width, width)
-            weight = jnp.concatenate([wq_ref[deep, :], wk_ref[deep, :], wv_ref[deep, :]], axis=1)
-            total += jnp.dot(block, weight, preferred_element_type=jnp.float32)
+            total += jnp.dot(block, w_ref[deep, :], preferred_element_type=jnp.float32)
             wide = block.astype(jnp.float32)
             squares += wide * wide
         mean = jnp.sum(squares, axis=1, keepdims=True) * (1.0 / (width * tensors))
@@ -177,14 +234,10 @@
         probability = (expo / jnp.sum(expo, axis=1, keepdims=True)).astype(jnp.bfloat16)
         heads = jnp.dot(probability, values, preferred_element_type=jnp.float32)
         heads_buf[unit, ten] = heads.astype(jnp.bfloat16)
-        for off in [o for d in range(tensors // 2, 0, -1) for o in sorted({d, tensors - d})]:
-            send(
-                heads_buf.at[unit, ten], heads_buf.at[unit, ten], s_h.at[unit], r_h.at[unit],
-                (rep, sec, lax.rem(ten + off, tensors)),
-            ).start()
+        near_and_far(heads_buf, unit, s_h, r_h)
 
     def stage_out(unit):
-        await_bytes(heads_buf.at[unit, pl.ds(0, tensors - 1)], r_h.at[unit])
+        await_rest(heads_buf, unit, r_h)
         total = x_buf[unit, ten].astype(jnp.float32)
         for b in range(0, tensors, 2):
             both = jnp.concatenate([heads_buf[unit, b], heads_buf[unit, b + 1]], axis=1)
@@ -199,72 +252,102 @@
                     (flip(spread(e, first_bits)), lax.rem(sec + 1, sections), ten),
                 ).start()
 
-    def tick(t, carry):
-        @pl.when((sec != 0) & (t < units))
-        def _():
-            stage_pick(t)
-
-        @pl.when((t >= 2) & (t < units + 2))
-        def _():
-            stage_attend(t - 2)
-
-        @pl.when(t < units)
-        def _():
-            stage_gather(t)
-
-        @pl.when(t >= 3)
-        def _():
-            stage_out(t - 3)
-
-        return carry
-
-    lax.fori_loop(0, units + 3, tick, 0)
+    stages = {
+        "pick": stage_pick, "gather": stage_gather, "hand_x": stage_hand_x,
+        "attend": stage_attend, "hand_heads": stage_hand_heads, "out": stage_out,
+    }
 
     piece = delta_buf.shape[1]
     per_head = HD // piece if piece <= HD else 1
     scale = inner_rate / math.sqrt(units * rows)
-
-    def delta_step(h, carry):
-        mine = heads_buf[:, h].reshape(units * rows, HD)
-        grad = lax.dot_general(
-            mine, grad_ref[...], (((0,), (0,)), ((), ())), preferred_element_type=jnp.float32
-        )
-        delta = (grad * scale).astype(jnp.bfloat16)
-        for q in range(per_head):
-            delta_buf[h * per_head + q] = delta[q * piece : (q + 1) * piece]
+    early = (0, units // 2, units - max(1, units // 8))
+
+    def add_up(start, stop, fresh, finish):
+        def head(h, carry):
+            count = stop - start
+            mine = heads_buf[pl.ds(start, count), h].reshape(count * rows, HD)
+            grad = lax.dot_general(
+                mine, grad_ref[pl.ds(start * rows, count * rows), :], (((0,), (0,)), ((), ())),
+                preferred_element_type=jnp.float32,
+            )
+            if not fresh:
+                grad = grad + grad_acc[h]
+            if finish:
+                delta = (grad * scale).astype(jnp.bfloat16)
+                for q in range(per_head):
+                    delta_buf[h * per_head + q] = delta[q * piece : (q + 1) * piece]
+            else:
+                grad_acc[h] = grad
+            return carry
+
+        lax.fori_loop(0, tensors, head, 0)
+
+    def tick(t, carry):
+        for name, late in SCHEDULE:
+            unit = t - late
+            due = (unit >= 0) & (unit < units)
+            if name == "pick":
+                due = due & (sec != 0)
+            pl.when(due)(functools.partial(stages[name], unit))
+
+        @pl.when((sec == 0) & (t == units // 2))
+        def _():
+            swap_turn(mom_a, mom_b, mom_d, r_ma, s_mb, r_mb)
+
+        done = t - dict(SCHEDULE)['out'] + 1
+        for start, stop in zip(early, early[1:]):
+            pl.when((sec == last) & (done == stop))(functools.partial(add_up, start, stop, start == 0, False))
         return carry
 
-    lax.fori_loop(0, tensors, delta_step, 0)
+    lax.fori_loop(0, units + max(late for _, late in SCHEDULE), tick, 0)
+
+    @pl.when(sec == last)
+    def _():
+        add_up(early[-1], units, False, True)
+
+    @pl.when(sec != last)
+    def _():
+        add_up(0, units, True, True)
+
     swap_start(delta_buf, del_a, s_da, r_da)
 
-    @pl.when(sec == 0)
-    def _():
-        swap_turn(mom_a, mom_b, mom_d, r_ma, s_mb, r_mb)
-
     swap_turn(del_a, del_b, del_d, r_da, s_db, r_db)
-    await_bytes(mom_d.at[pl.ds(1, replicas - 1)], r_mb)
-    await_bytes(del_d.at[pl.ds(1, replicas - 1)], r_db)
-
-    def update(c, carry):
+    for p in range(PARTS):
+        await_part(mom_d, p, r_mb)
+
+    def update(p, c):
+        span = rows_of(p)
         there = jnp.bitwise_xor(pair, c)
-        mean_delta = 0.5 * (delta_buf[c].astype(jnp.float32) + del_d[there].astype(jnp.float32))
-        both = mom_ref[c].astype(jnp.float32) + mom_d[there].astype(jnp.float32)
+        mean_delta = 0.5 * (delta_buf[c, span].astype(jnp.float32) + del_d[there, span].astype(jnp.float32))
+        both = mom_ref[c, span].astype(jnp.float32) + mom_d[there, span].astype(jnp.float32)
         momentum_next = outer_beta * 0.5 * both + mean_delta
-        old = wo_ref[pl.ds(pl.multiple_of(c * piece, piece), piece), :].astype(jnp.float32)
-        slow_ref[c] = (old - outer_rate * (outer_beta * momentum_next + mean_delta)).astype(jnp.bfloat16)
-        newm_ref[c] = momentum_next.astype(jnp.bfloat16)
+        old = wo_ref[pl.ds(pl.multiple_of(c * piece + p * part, part), part), :].astype(jnp.float32)
+        slow_ref[c, span] = (old - outer_rate * (outer_beta * momentum_next + mean_delta)).astype(jnp.bfloat16)
+        newm_ref[c, span] = momentum_next.astype(jnp.bfloat16)
+
+    for p in range(PARTS):
+        await_part(del_d, p, r_db)
+
+    def update_all(c, carry):
+        for p in range(PARTS):
+            update(p, c)
         return carry
 
-    lax.fori_loop(0, replicas, update, 0)
-
-    await_bytes(mom_a.at[pl.ds(1, replicas - 1)], s_ma)
-    await_bytes(mom_a.at[pl.ds(1, replicas - 1)], s_mb)
-    await_bytes(mom_a.at[pl.ds(1, replicas - 1)], s_da)
-    await_bytes(mom_a.at[pl.ds(1, replicas - 1)], s_db)
+    lax.fori_loop(0, replicas, update_all, 0)
+
+    for p in range(PARTS):
+        await_part(mom_d, p, s_ma)
+    for p in range(PARTS):
+        await_part(mom_d, p, s_mb)
+    for p in range(PARTS):
+        await_part(mom_d, p, s_da)
+    for p in range(PARTS):
+        await_part(mom_d, p, s_db)
 
     def drain(u, carry):
-        await_bytes(x_buf.at[u, pl.ds(0, tensors - 1)], s_x.at[u])
-        await_bytes(heads_buf.at[u, pl.ds(0, tensors - 1)], s_h.at[u])
+        for kind, blocks in ((0, 2), (1, 2), (2, 3)):
+            await_bytes(x_buf.at[u, pl.ds(0, blocks)], s_x.at[u, kind])
+            await_bytes(heads_buf.at[u, pl.ds(0, blocks)], s_h.at[u, kind])
 
         @pl.when(sec != 0)
         def _():
@@ -296,6 +379,7 @@
     dma = pltpu.SemaphoreType.DMA
     vmem = pl.BlockSpec(memory_space=pltpu.VMEM)
     smem = pl.BlockSpec(memory_space=pltpu.SMEM)
+    hbm = pl.BlockSpec(memory_space=pl.ANY)
     cfg = (replicas, sections, tensors, units, chunks, rows)
     out, slow, newm = pl.pallas_call(
         functools.partial(kernel, cfg),
@@ -304,21 +388,31 @@
             jax.ShapeDtypeStruct((replicas, piece, width), bf),
             jax.ShapeDtypeStruct((replicas, piece, width), bf),
         ),
-        in_specs=[smem, smem] + [vmem] * 8,
+        in_specs=[smem, smem] + [hbm] * 8,
         out_specs=(vmem, vmem, vmem),
         scratch_shapes=[
+            pltpu.VMEM(positions.shape, jnp.int32),
+            pltpu.VMEM((units, rows, width), bf),
+            pltpu.VMEM((width * tensors, 3 * HD), bf),
+            pltpu.VMEM(wo.shape, bf),
+            swap,
+            pltpu.VMEM((units * rows, width), bf),
+            pltpu.VMEM((tensors, HD, width), jnp.float32),
             pltpu.VMEM((units, n_first, rows, width), bf),
             pltpu.VMEM((units, n_second, rows, width), bf),
             pltpu.VMEM((units, tensors, rows, width), bf),
             pltpu.VMEM((units, tensors, rows, HD), bf),
             pltpu.VMEM((micros, chunks, rows, HD), bf),
             pltpu.VMEM((micros, chunks, rows, HD), bf),
-            swap, swap, swap, swap, swap, swap, swap,
+            swap, swap, swap, swap, swap,
+            [pltpu.VMEM((replicas, piece // PARTS, width), bf)] * (2 * PARTS),
         ]
-        + [dma((units,))] * 8
-        + [dma] * 8,
+        + [dma((units,))] * 4
+        + [dma((units, 3))] * 4
+        + [dma((PARTS,))] * 8
+        + [dma((8,))],
         compiler_params=pltpu.CompilerParams(
-            collective_id=0, has_side_effects=True, vmem_limit_bytes=40 * 1024 * 1024
+            collective_id=0, has_side_effects=True, vmem_limit_bytes=58 * 1024 * 1024
         ),
     )(
         route_keys, gossip_partner, positions, tokens.reshape(units, rows, width),

time: 222 us -> 187 us (0.84)
  Pallas kernels: 210 us -> 181 us
  local copies, waits for them, and re-layouts: 10.9 us -> 5.09 us
    pallas_call x1, Pallas kernels: 210 us -> 181 us  [shards(): pl.pallas_call(functools.partial(kernel, cfg), out_shape=(jax.ShapeDtypeS...]
    unnamed x24 -> x10, local copies, waits for them, and re-layouts: 10.9 us -> 5.09 us
where the time goes in v2:
time: 187 us; the launch traced here: 186 us
  Pallas kernels  181 us (97%)
  local copies, waits for them, and re-layouts  5.09 us (3%)
    pallas_call x1, Pallas kernels, shards(): pl.pallas_call(functools.partial(kernel, cfg), out_shape=(jax.ShapeDtypeS...  181 us
    unnamed x10, local copies, waits for them, and re-layouts  5.09 us

profile of v2, /device:TPU:193, one launch (start us, length us, event | category | flops | bytes accessed | tf_op | source)
XLA Modules:
  0.0 186.5 jit_solution(8445196066418632506)
XLA Ops:
  0.6 0.0 copy-start.2
  0.6 0.7 copy-done.2
  1.3 0.7 copy.13.route_ref
  2.0 180.7 %shard_map.121 = (bf16[16,32,256]{2,1,0:T(8,128)(2,1)}, bf16[16,64,256]{2,1,0:T(8,128)(2,1)}, bf16[16,64,256]{2,1,0:T(8,128)(2,1)}) custom-call(s32[3,2]{1,0:T(4,128)} %copy.13.route_ref, s32[4,16]{1,0:T(4,128)} %gossip_ref.1, s32[16,2,256]{2,1,0:T(2,128)} %pos_in.1, bf16[16,32,256]{2,1,0:T(8,128)(2,1)} %bitcast.17, bf16[2048,128]{1,0:T(8,128)(2,1)} %bitcast.10, ...), custom_call_target="tpu_custom_call" | custom-call | tf_op jit(solution)/shard_map/pallas_call | solution.py:384
  182.7 0.0 copy-start.1
  182.7 1.7 copy.17
  184.5 0.0 copy-done.1
  184.5 0.0 copy-start
  184.5 0.8 copy.18
  185.3 0.4 copy-done
  185.7 0.8 copy.19
Async XLA Ops:
  0.6 0.7 copy-start.2
  182.7 1.7 copy-start.1
  184.5 1.2 copy-start

commit v3 on v2

--- a/solution.py
+++ b/solution.py
@@ -47,7 +47,7 @@
     first_buf, second_buf, x_buf, heads_buf, k_buf, v_buf,
     delta_buf, mom_b, mom_d, del_b, del_d, landed,
     s_first, r_first, s_second, r_second, s_x, r_x, s_h, r_h,
-    s_ma, r_ma, s_mb, r_mb, s_da, r_da, s_db, r_db, s_in,
+    s_ma, r_ma, s_mb, r_mb, s_da, r_da, s_db, r_db, s_in, go,
 ):
     replicas, sections, tensors, units, chunks, rows = cfg
     mom_a, del_a = landed[:PARTS], landed[PARTS:]
@@ -282,6 +282,9 @@
 
         lax.fori_loop(0, tensors, head, 0)
 
+    def pass_go():
+        pl.semaphore_signal(go, inc=1, device_id=(rep, lax.rem(sec + last, sections), ten), device_id_type=MESH)
+
     def tick(t, carry):
         for name, late in SCHEDULE:
             unit = t - late
@@ -294,6 +297,10 @@
         def _():
             swap_turn(mom_a, mom_b, mom_d, r_ma, s_mb, r_mb)
 
+        @pl.when((sec == last) & (t == units - 1))
+        def _():
+            pass_go()
+
         done = t - dict(SCHEDULE)['out'] + 1
         for start, stop in zip(early, early[1:]):
             pl.when((sec == last) & (done == stop))(functools.partial(add_up, start, stop, start == 0, False))
@@ -308,6 +315,14 @@
     @pl.when(sec != last)
     def _():
         add_up(0, units, True, True)
+
+    @pl.when(sec != last)
+    def _():
+        pl.semaphore_wait(go, 1)
+
+    @pl.when((sec != last) & (sec != 0))
+    def _():
+        pass_go()
 
     swap_start(delta_buf, del_a, s_da, r_da)
 
@@ -410,9 +425,9 @@
         + [dma((units,))] * 4
         + [dma((units, 3))] * 4
         + [dma((PARTS,))] * 8
-        + [dma((8,))],
+        + [dma((8,)), pltpu.SemaphoreType.REGULAR],
         compiler_params=pltpu.CompilerParams(
-            collective_id=0, has_side_effects=True, vmem_limit_bytes=58 * 1024 * 1024
+            collective_id=0, has_side_effects=True, vmem_limit_bytes=52 * 1024 * 1024
         ),
     )(
         route_keys, gossip_partner, positions, tokens.reshape(units, rows, width),

time: 187 us -> 178 us (0.952)
  Pallas kernels: 181 us -> 171 us
    pallas_call x1, Pallas kernels: 181 us -> 171 us  [shards(): pl.pallas_call(functools.partial(kernel, cfg), out_shape=(jax.ShapeDtypeS...]
    unnamed x10 -> x14, local copies, waits for them, and re-layouts: 5.09 us -> 5.71 us
where the time goes in v3:
time: 178 us
  Pallas kernels  171 us (96%)
  local copies, waits for them, and re-layouts  5.71 us (3%)
    pallas_call x1, Pallas kernels, shards(): pl.pallas_call(functools.partial(kernel, cfg), out_shape=(jax.ShapeDtypeS...  171 us
    unnamed x14, local copies, waits for them, and re-layouts  5.71 us

profile of v3, /device:TPU:193, one launch (start us, length us, event | category | flops | bytes accessed | tf_op | source)
XLA Modules:
  0.0 177.8 jit_solution(11386727654897451034)
XLA Ops:
  0.6 0.0 copy-start.4
  0.6 0.0 copy-start.3
  0.7 0.7 copy-done.4
  1.3 0.1 copy.13.route_ref
  1.4 0.0 copy-done.3
  1.4 0.0 copy-start
  1.4 0.9 copy-done
  2.4 0.0 copy-start.1
  2.4 0.9 copy-done.1
  3.3 0.0 copy-start.2
  3.3 0.8 copy-done.2
  4.1 171.4 %shard_map.121 = (bf16[16,32,256]{2,1,0:T(8,128)(2,1)S(1)}, bf16[16,64,256]{2,1,0:T(8,128)(2,1)S(1)}, bf16[16,64,256]{2,1,0:T(8,128)(2,1)S(1)}) custom-call(s32[3,2]{1,0:T(4,128)S(1)} %copy.13.route_ref, s32[4,16]{1,0:T(4,128)S(1)} %copy-done.3, s32[16,2,256]{2,1,0:T(2,128)S(1)} %copy-done.2, bf16[16,32,256]{2,1,0:T(8,128)(2,1)S(1)} %bitcast.12, ...), custom_call_target="tpu_custom_call" | custom-call | tf_op jit(solution)/shard_map/pallas_call | solution.py:399
  175.5 0.7 copy.17
  176.2 0.8 copy.18
  177.0 0.8 copy.19
Async XLA Ops:
  0.6 0.7 copy-start.4
  0.6 0.8 copy-start.3
  1.4 1.0 copy-start
  2.4 0.9 copy-start.1
  3.3 0.8 copy-start.2

commit v4 on v3

--- a/solution.py
+++ b/solution.py
@@ -145,7 +145,7 @@
         swap_turn(mom_a, mom_b, mom_d, r_ma, s_mb, r_mb)
 
     def relay_mask(unit):
-        return route_ref[jnp.maximum(sec - 1, 0), unit // chunks]
+        return route_ref[unit // chunks, jnp.maximum(sec - 1, 0)]
 
     def beside(off):
         return lax.rem(ten + off + tensors, tensors)
@@ -201,7 +201,7 @@
         micro, chunk = unit // chunks, lax.rem(unit, chunks)
         anchor = rep
         for earlier in range(last):
-            anchor = jnp.bitwise_xor(anchor, jnp.where(earlier < sec, route_ref[earlier, micro], 0))
+            anchor = jnp.bitwise_xor(anchor, jnp.where(earlier < sec, route_ref[micro, earlier], 0))
         await_rest(x_buf, unit, r_x)
         width = x_buf.shape[3]
         total = jnp.zeros((rows, 3 * HD), jnp.float32)
@@ -297,7 +297,7 @@
         def _():
             swap_turn(mom_a, mom_b, mom_d, r_ma, s_mb, r_mb)
 
-        @pl.when((sec == last) & (t == units - 1))
+        @pl.when((sec == last) & (t == units - 2))
         def _():
             pass_go()
 
@@ -430,7 +430,7 @@
             collective_id=0, has_side_effects=True, vmem_limit_bytes=52 * 1024 * 1024
         ),
     )(
-        route_keys, gossip_partner, positions, tokens.reshape(units, rows, width),
+        route_keys.T, gossip_partner, positions, tokens.reshape(units, rows, width),
         query_weight[0, 0], key_weight[0, 0], value_weight[0, 0], wo,
         momentum.reshape(replicas, piece, width), out_grad.reshape(units * rows, width),
     )

time: 178 us -> 178 us (level)
    unnamed x14 -> x13, local copies, waits for them, and re-layouts: 5.71 us -> 5.63 us
where the time goes in v4:
time: 178 us
  Pallas kernels  171 us (96%)
  local copies, waits for them, and re-layouts  5.63 us (3%)
    pallas_call x1, Pallas kernels, shards(): pl.pallas_call(functools.partial(kernel, cfg), out_shape=(jax.ShapeDtypeS...  171 us
    unnamed x13, local copies, waits for them, and re-layouts  5.63 us

profile of v4, /device:TPU:193, one launch (start us, length us, event | category | flops | bytes accessed | tf_op | source)
XLA Modules:
  0.0 177.5 jit_solution(11282508411983213675)
XLA Ops:
  0.6 0.0 copy-start.3
  0.6 0.0 copy-start.4
  0.7 0.7 copy-done.3
  1.3 0.0 copy-done.4
  1.3 0.0 copy-start
  1.3 0.9 copy-done
  2.3 0.0 copy-start.1
  2.3 0.9 copy-done.1
  3.2 0.0 copy-start.2
  3.2 0.8 copy-done.2
  4.0 171.2 %shard_map.121 = (bf16[16,32,256]{2,1,0:T(8,128)(2,1)S(1)}, bf16[16,64,256]{2,1,0:T(8,128)(2,1)S(1)}, bf16[16,64,256]{2,1,0:T(8,128)(2,1)S(1)}) custom-call(s32[2,3]{1,0:T(2,128)S(1)} %bitcast.16, s32[4,16]{1,0:T(4,128)S(1)} %copy-done.3, s32[16,2,256]{2,1,0:T(2,128)S(1)} %copy-done.2, bf16[16,32,256]{2,1,0:T(8,128)(2,1)S(1)} %bitcast.13, ...), custom_call_target="tpu_custom_call" | custom-call | tf_op jit(solution)/shard_map/pallas_call | solution.py:399
  175.2 0.7 copy.16
  175.9 0.8 copy.17
  176.7 0.8 copy.18
Async XLA Ops:
  0.6 0.7 copy-start.3
  0.6 0.7 copy-start.4
  1.3 0.9 copy-start
  2.3 0.9 copy-start.1
  3.2 0.8 copy-start.2
